TPU v7x, 256 devices: a whole 4x4x8 slice. The times are simulated.
256 devices in a mesh: grp: 8 (over y, core), dev: 32 (over z, x).
Axes of the slice: x: 4, y: 4, z: 8, core: 2. Of those that a mesh axis runs over, the one named last changes fastest.
Arguments:
- signals: float32 [256, 32, 128], P(('grp', 'dev')), may hold values from -6 to 6
- maps: bfloat16 [256, 16, 256, 128], P(('grp', 'dev')), may hold values from -0.01171875 to 0.01171875
- uses: int32 [256, 16], P(('grp', 'dev')), may hold values from 0 to 31, all different within a row; in each aligned block of 32 rows (0 to 31, 32 to 63, ...) at most 20 rows name the same one
- owner: int32 [32], replicated, may hold values from 0 to 31, each once
- local_dict: float32 [8, 32, 64, 32, 256], P('grp', 'dev'), may hold values from -45 to 45
- duals: float32 [8, 32, 64, 32, 256], P('grp', 'dev'), may hold values from -4 to 4
- consensus: float32 [32, 64, 32, 256], P('dev'), may hold values from -6 to 6
Outputs:
- consensus_final: float32 [32, 64, 32, 256], P('dev')
- duals_final: float32 [8, 32, 64, 32, 256], P('grp', 'dev')
- residual: float32 [256, 32, 128], P(('grp', 'dev'))
Inputs may be any that keep to these rules, and one draw needn't show every extreme that they name: `uses`: each window names 16 different classes; among the windows of one group at most 20 name one class, and in every draw some class of some group is named by exactly 20 windows. `owner`: each slot holds exactly one class.
All inputs are finite; a program needn't handle non-finite values.
Results may differ from a plain program's by a relative error of at most 0.0053.
Values may be sent and summed in bfloat16 or wider, within the bound.
A program may use at most 128 MiB of HBM per device.

v0:
```python
import math

import jax
import jax.numpy as jnp
from jax import lax
from jax.sharding import PartitionSpec as P

ITERS = 2


step_size = 4.0
penalty = 1.0


def shift_sum(values):
    tap_count = values.shape[0]
    time_len = values.shape[-1]
    widths = [(0, 0)] * (values.ndim - 1) + [(tap_count, 0)]
    padded = jnp.pad(values, widths)
    summed = jnp.zeros(values.shape[1:], jnp.float32)
    for lag in range(tap_count):
        summed = summed + padded[lag, ..., tap_count - lag : tap_count - lag + time_len]
    return summed


def shift_stack(source, tap_count):
    time_len = source.shape[-1]
    widths = [(0, 0)] * (source.ndim - 1) + [(0, tap_count)]
    padded = jnp.pad(source, widths)
    return jnp.stack([padded[..., lag : lag + time_len] for lag in range(tap_count)])


def project(values):
    count = values.shape[-3] * values.shape[-2]
    norms = jnp.sqrt(jnp.sum(values * values, axis=(-3, -2), keepdims=True))
    return values / jnp.maximum(1.0, norms / math.sqrt(count))


def local(signals, maps, uses, owner, local_dict, duals, consensus):
    dev_count = lax.axis_size("dev")
    grp_count = lax.axis_size("grp")
    capacity = 5 * dev_count // 8
    class_count = owner.shape[0]
    use_row = uses[0]
    class_pick = (use_row[:, None] == jnp.arange(class_count, dtype=jnp.int32)[None, :]).astype(
        jnp.int32
    )
    owner_slot = jnp.sum(class_pick * owner[None, :], axis=1)
    send_mask = owner_slot[:, None] == jnp.arange(dev_count, dtype=jnp.int32)[None, :]
    send_maps = jnp.einsum(
        "ud,uft->dft", send_mask.astype(jnp.bfloat16), maps[0], preferred_element_type=jnp.float32
    ).astype(jnp.bfloat16)
    use_flags = jnp.sum(send_mask.astype(jnp.int32), axis=0)
    got_maps, got_flags = (
        lax.all_to_all(send_maps, "dev", split_axis=0, concat_axis=0, tiled=True),
        lax.all_to_all(use_flags, "dev", split_axis=0, concat_axis=0, tiled=True),
    )
    slot_rank = jnp.cumsum(got_flags) - got_flags
    select = (slot_rank[None, :] == jnp.arange(capacity, dtype=jnp.int32)[:, None]) & (
        got_flags[None, :] > 0
    )
    held_maps = jnp.einsum(
        "ks,sft->fkt", select.astype(jnp.bfloat16), got_maps, preferred_element_type=jnp.float32
    ).astype(jnp.bfloat16)
    filt_count = held_maps.shape[0]
    time_len = held_maps.shape[2]
    held_flat = held_maps.reshape(filt_count, capacity * time_len)
    select_f = select.astype(jnp.float32)
    send_live = (use_flags > 0).astype(jnp.float32)
    dict_now = local_dict[0, 0]
    dual_now = duals[0, 0]
    cons_now = consensus[0]
    tap_count = dict_now.shape[0]
    chan_count = dict_now.shape[1]
    residual_now = signals[0]
    for iteration in range(ITERS):
        dict_bf = dict_now.astype(jnp.bfloat16).reshape(tap_count * chan_count, filt_count)
        spread = jnp.dot(dict_bf, held_flat, preferred_element_type=jnp.float32).reshape(
            tap_count, chan_count, capacity, time_len
        )
        pieces = shift_sum(spread)
        outgoing = jnp.einsum("ks,ckt->sct", select_f, pieces, precision=lax.Precision.HIGHEST)
        incoming = lax.all_to_all(outgoing, "dev", split_axis=0, concat_axis=0, tiled=True)
        residual_now = signals[0] - jnp.sum(incoming, axis=0)
        residual_out = send_live[:, None, None] * residual_now[None]
        residual_in = lax.all_to_all(
            residual_out.astype(jnp.bfloat16), "dev", split_axis=0, concat_axis=0, tiled=True
        ).astype(residual_out.dtype)
        residual_held = jnp.einsum(
            "ks,sct->ckt", select_f, residual_in, precision=lax.Precision.HIGHEST
        ).astype(jnp.bfloat16)
        lagged = shift_stack(residual_held, tap_count).reshape(
            tap_count * chan_count, capacity * time_len
        )
        gradient = lax.dot_general(
            lagged, held_flat, (((1,), (1,)), ((), ())), preferred_element_type=jnp.float32
        )
        gradient = gradient.reshape(tap_count, chan_count, filt_count)
        new_dict = (dict_now + step_size * gradient + penalty * (cons_now - dual_now)) / (
            1.0 + penalty
        )
        averaged_in = (new_dict + dual_now)[None, None]
        summed = lax.psum(averaged_in, "grp")
        cons_new = project(summed / grp_count)
        cons_new = cons_new[0, 0]
        dual_now = dual_now + new_dict - cons_new
        dict_now = new_dict
        cons_now = cons_new
    return (cons_now[None], dual_now[None, None], residual_now[None])


def solution(mesh):
    placed = (
        P(("grp", "dev"), None, None),
        P(("grp", "dev"), None, None, None),
        P(("grp", "dev"), None),
        P(),
        P("grp", "dev", None, None, None),
        P("grp", "dev", None, None, None),
        P("dev", None, None, None),
    )
    return jax.shard_map(
        local,
        mesh=mesh,
        in_specs=placed,
        out_specs=(
            P("dev", None, None, None),
            P("grp", "dev", None, None, None),
            P(("grp", "dev"), None, None),
        ),
        check_vma=False,
    )
```

profile of v0, /device:TPU:2, one launch (start us, length us, event | category | flops | bytes accessed | tf_op | source)
XLA Modules:
  0.0 473.0 jit_solution(10624503554403230192)
XLA Ops:
  7.2 0.9 select_reduce_fusion
  8.9 11.6 %all-to-all-start = ((s32[32,1,1]{2,1,0:T(1,128)}), s32[32,1,1]{2,1,0:T(1,128)S(1)}, u32[]{:S(2)}, u32[]{:S(2)}) async-start(s32[32,1,1]{2,1,0:T(1,128)} %copy.54), calls=%async_computation | async-start | bytes 32768 | tf_op jit(solution)/shard_map/all_to_all | solution.py:56
  20.5 1.0 convolution_convert_fusion
  21.6 2.1 copy.57
  23.7 5.3 %all-to-all-done = s32[32,1,1]{2,1,0:T(1,128)S(1)} async-done(((s32[32,1,1]{2,1,0:T(1,128)}), s32[32,1,1]{2,1,0:T(1,128)S(1)}, u32[]{:S(2)}, u32[]{:S(2)}) %all-to-all-start) | async-done | bytes 160 | tf_op jit(solution)/shard_map/all_to_all | solution.py:56
  29.0 5.1 %all-to-all-start.1 = ((bf16[32,256,128]{2,1,0:T(8,128)(2,1)}), bf16[32,256,128]{2,1,0:T(8,128)(2,1)S(1)}, u32[]{:S(2)}, u32[]{:S(2)}) async-start(bf16[32,256,128]{2,1,0:T(8,128)(2,1)} %copy.57), calls=%async_computation.1 | async-start | bytes 4194304 | tf_op jit(solution)/shard_map/all_to_all | solution.py:55
  34.1 1.7 convert_element_type.64
  36.7 46.0 %all-to-all-done.1 = bf16[32,256,128]{2,1,0:T(8,128)(2,1)S(1)} async-done(((bf16[32,256,128]{2,1,0:T(8,128)(2,1)}), bf16[32,256,128]{2,1,0:T(8,128)(2,1)S(1)}, u32[]{:S(2)}, u32[]{:S(2)}) %all-to-all-start.1) | async-done | bytes 2097184 | tf_op jit(solution)/shard_map/all_to_all | solution.py:55
  82.8 2.5 fusion.22
  85.3 2.0 copy.59
  87.3 8.6 %convolution_bitcast_fusion = f32[2048,2560]{1,0:T(8,128)} fusion(bf16[256,2560]{0,1:T(8,128)(2,1)S(1)} %bitcast.1581, bf16[2048,256]{1,0:T(8,128)(2,1)S(1)} %bitcast.1583), kind=kOutput, calls=%fused_computation.126 | convolution fusion | flops 2684354560 | bytes 23330816 | tf_op jit(solution)/shard_map/dot_general | solution.py:78
  95.9 24.1 %reshape.115 = f32[64,32,20,128]{3,2,1,0:T(8,128)} reshape(f32[2048,2560]{1,0:T(8,128)} %convolution_bitcast_fusion) | data formatting | bytes 41943040 | tf_op jit(solution)/shard_map/reshape | solution.py:78
  120.1 11.8 %fusion.163 = f32[32,32,128]{2,0,1:T(8,128)S(1)} fusion(f32[64,32,20,128]{3,2,1,0:T(8,128)} %reshape.115, f32[32,20,128]{2,1,0:T(8,128)S(1)} %squeeze.396, s32[32]{0:T(128)S(1)} %sub.27, pred[32]{0:T(512)(128)(4,1)S(1)} %broadcast_compare_fusion), kind=kOutput, calls=%fused_computation.423 | convolution fusion | flops 36619520 | bytes 21823648 | tf_op jit(solution)/shard_map/ks,ckt->sct/dot_general | solution.py:82
  132.0 1.1 copy.60
  133.0 6.7 %all-to-all-start.2 = ((f32[32,32,128]{2,1,0:T(8,128)}), f32[32,32,128]{2,1,0:T(8,128)S(1)}, u32[]{:S(2)}, u32[]{:S(2)}) async-start(f32[32,32,128]{2,1,0:T(8,128)} %copy.60), calls=%async_computation.2 | async-start | bytes 1048576 | tf_op jit(solution)/shard_map/all_to_all | solution.py:83
  139.7 14.8 %all-to-all-done.2 = f32[32,32,128]{2,1,0:T(8,128)S(1)} async-done(((f32[32,32,128]{2,1,0:T(8,128)}), f32[32,32,128]{2,1,0:T(8,128)S(1)}, u32[]{:S(2)}, u32[]{:S(2)}) %all-to-all-start.2) | async-done | bytes 524320 | tf_op jit(solution)/shard_map/all_to_all | solution.py:83
  154.7 15.2 %all_to_all.31 = bf16[32,32,128]{2,1,0:T(8,128)(2,1)S(1)} all-to-all(bf16[32,32,128]{2,1,0:T(8,128)(2,1)S(1)} %multiply_convert_fusion.1), channel_id=1, replica_groups=mesh['grp'=8,'dev'=32] {'dev'}, dimensions={0} | all-to-all | bytes 524288 | tf_op jit(solution)/shard_map/all_to_all | solution.py:86
  221.6 8.8 %fusion.10 = f32[64,32,256]{2,1,0:T(8,128)S(1)} fusion(f32[1,1,64,32,256]{4,3,2,1,0:T(8,128)S(1)} %copy-done.6, f32[1,64,32,256]{3,2,1,0:T(8,128)S(1)} %copy-done.12, f32[1,1,64,32,256]{4,3,2,1,0:T(8,128)S(1)} %copy-done.8, bf16[64,32,20,128]{3,2,1,0:T(8,128)(2,1)} %constant_dynamic-update-slice_fusion, bf16[256,20,128]{2,1,0:T(8,128)(2,1)S(1)} %copy-done.4), kind=kOutput, calls=%fused_computation.269 | convolution fusion | flops 2686976000 | bytes 20185088 | tf_op jit(solution)/shard_map/dot_general | solution.py:95
  230.5 2.9 fusion.25
  233.4 5.5 %fusion.274 = f32[32,20,128]{2,0,1:T(8,128)S(1)} fusion(f32[64,32,20,128]{3,1,2,0:T(8,128)S(1)} %fusion.25), kind=kLoop, calls=%fused_computation.533 | loop fusion | flops 5160960 | bytes 21626880 | tf_op jit(solution)/shard_map/add | solution.py:22
  239.5 1.1 copy.65
  240.6 5.8 %all-to-all-start.4 = ((f32[32,32,128]{2,1,0:T(8,128)}), f32[32,32,128]{2,1,0:T(8,128)S(1)}, u32[]{:S(2)}, u32[]{:S(2)}) async-start(f32[32,32,128]{2,1,0:T(8,128)} %copy.65), calls=%async_computation.4 | async-start | bytes 1048576 | tf_op jit(solution)/shard_map/all_to_all | solution.py:83
  246.4 3.3 fusion.14
  249.8 9.9 %all-to-all-done.4 = f32[32,32,128]{2,1,0:T(8,128)S(1)} async-done(((f32[32,32,128]{2,1,0:T(8,128)}), f32[32,32,128]{2,1,0:T(8,128)S(1)}, u32[]{:S(2)}, u32[]{:S(2)}) %all-to-all-start.4) | async-done | bytes 524320 | tf_op jit(solution)/shard_map/all_to_all | solution.py:83
  260.5 5.6 %all-to-all-start.5 = ((bf16[32,32,128]{2,1,0:T(8,128)(2,1)}), bf16[32,32,128]{2,1,0:T(8,128)(2,1)S(1)}, u32[]{:S(2)}, u32[]{:S(2)}) async-start(bf16[32,32,128]{2,1,0:T(8,128)(2,1)} %multiply_convert_fusion), calls=%async_computation.5 | async-start | bytes 524288 | tf_op jit(solution)/shard_map/all_to_all | solution.py:86
  266.4 56.0 %all-reduce.7.cloned.1.call-done = f32[1,1,64,32,256]{4,3,2,1,0:T(8,128)} async-done(((f32[1,1,64,32,256]{4,3,2,1,0:T(8,128)}), f32[1,1,64,32,256]{4,3,2,1,0:T(8,128)}) %all-reduce.7.cloned.1.call-update) | async-done | bytes 2097168 | tf_op jit(solution)/shard_map/psum | solution.py:103
  322.4 1.9 multiply_reduce_fusion.1
  376.0 9.6 %fusion.7 = f32[64,32,256]{2,1,0:T(8,128)} fusion(f32[64,32,256]{2,1,0:T(8,128)S(1)} %fusion.10, f32[1,1,64,32,256]{4,3,2,1,0:T(8,128)S(1)} %copy-done.7, f32[1,1,64,32,256]{4,3,2,1,0:T(8,128)S(1)} %copy-done.9, bf16[64,32,20,128]{3,2,1,0:T(8,128)(2,1)} %constant_dynamic-update-slice_fusion.64, f32[256]{0:T(256)S(1)} %multiply_maximum_fusion.1, ...), kind=kOutput, calls=%fused_computation.263 | convolution fusion | flops 2689597440 | bytes 20186112 | tf_op jit(solution)/shard_map/dot_general | solution.py:95
  385.7 70.6 %all-reduce.9.cloned.1.call-done = f32[1,1,64,32,256]{4,3,2,1,0:T(8,128)} async-done(((f32[1,1,64,32,256]{4,3,2,1,0:T(8,128)}), f32[1,1,64,32,256]{4,3,2,1,0:T(8,128)}) %all-reduce.9.cloned.1.call-update) | async-done | bytes 2097168 | tf_op jit(solution)/shard_map/psum | solution.py:103
  456.3 1.9 multiply_reduce_fusion
  458.2 4.2 fusion.4
  462.4 3.3 fusion.34
  (179 shorter events, 107.0 us)
Async XLA Ops:
  7.2 13.4 %copy-start = (bf16[1,16,256,128]{3,2,1,0:T(8,128)(2,1)S(1)}, bf16[1,16,256,128]{3,2,1,0:T(8,128)(2,1)}, u32[]{:S(2)}) copy-start(bf16[1,16,256,128]{3,2,1,0:T(8,128)(2,1)} %param.8) | copy-start | bytes 3145732
  8.9 20.1 %all-to-all-start = ((s32[32,1,1]{2,1,0:T(1,128)}), s32[32,1,1]{2,1,0:T(1,128)S(1)}, u32[]{:S(2)}, u32[]{:S(2)}) async-start(s32[32,1,1]{2,1,0:T(1,128)} %copy.54), calls=%async_computation | async-start | bytes 32768 | tf_op jit(solution)/shard_map/all_to_all | solution.py:56
  29.0 53.8 %all-to-all-start.1 = ((bf16[32,256,128]{2,1,0:T(8,128)(2,1)}), bf16[32,256,128]{2,1,0:T(8,128)(2,1)S(1)}, u32[]{:S(2)}, u32[]{:S(2)}) async-start(bf16[32,256,128]{2,1,0:T(8,128)(2,1)} %copy.57), calls=%async_computation.1 | async-start | bytes 4194304 | tf_op jit(solution)/shard_map/all_to_all | solution.py:55
  87.3 8.6 %copy-start.2 = (bf16[256,20,128]{0,2,1:T(8,128)(2,1)}, bf16[256,20,128]{0,2,1:T(8,128)(2,1)S(1)}, u32[]{:S(2)}) copy-start(bf16[256,20,128]{0,2,1:T(8,128)(2,1)S(1)} %copy.59) | copy-start | bytes 3932164
  95.9 24.1 %slice-start = ((f32[2048,2560]{1,0:T(8,128)}), f32[32,2560]{1,0:T(8,128)S(1)}, s32[]{:S(2)}) async-start(f32[2048,2560]{1,0:T(8,128)} %convolution_bitcast_fusion), calls=%async_computation.8 | async-start | bytes 655360 | tf_op jit(solution)/shard_map/slice | solution.py:22
  120.1 34.5 %copy-start.10 = (f32[1,32,128]{2,1,0:T(8,128)S(1)}, f32[1,32,128]{2,1,0:T(8,128)}, u32[]{:S(2)}) copy-start(f32[1,32,128]{2,1,0:T(8,128)} %param.7) | copy-start | bytes 49156
  133.0 21.5 %all-to-all-start.2 = ((f32[32,32,128]{2,1,0:T(8,128)}), f32[32,32,128]{2,1,0:T(8,128)S(1)}, u32[]{:S(2)}, u32[]{:S(2)}) async-start(f32[32,32,128]{2,1,0:T(8,128)} %copy.60), calls=%async_computation.2 | async-start | bytes 1048576 | tf_op jit(solution)/shard_map/all_to_all | solution.py:83
  169.9 51.7 %copy-start.4 = (bf16[256,20,128]{2,1,0:T(8,128)(2,1)S(1)}, bf16[256,20,128]{2,1,0:T(8,128)(2,1)}, u32[]{:S(2)}) copy-start(bf16[256,20,128]{2,1,0:T(8,128)(2,1)} %fusion.22) | copy-start | bytes 3932164
  169.9 51.7 %copy-start.6 = (f32[1,1,64,32,256]{4,3,2,1,0:T(8,128)S(1)}, f32[1,1,64,32,256]{4,3,2,1,0:T(8,128)}, u32[]{:S(2)}) copy-start(f32[1,1,64,32,256]{4,3,2,1,0:T(8,128)} %param.12) | copy-start | bytes 6291460
  169.9 51.7 %copy-start.8 = (f32[1,1,64,32,256]{4,3,2,1,0:T(8,128)S(1)}, f32[1,1,64,32,256]{4,3,2,1,0:T(8,128)}, u32[]{:S(2)}) copy-start(f32[1,1,64,32,256]{4,3,2,1,0:T(8,128)} %param.11) | copy-start | bytes 6291460
  169.9 51.7 %copy-start.12 = (f32[1,64,32,256]{3,2,1,0:T(8,128)S(1)}, f32[1,64,32,256]{3,2,1,0:T(8,128)}, u32[]{:S(2)}) copy-start(f32[1,64,32,256]{3,2,1,0:T(8,128)} %param.13) | copy-start | bytes 6291460
  221.6 8.9 %copy-start.3 = (bf16[256,20,128]{0,2,1:T(8,128)(2,1)S(1)}, bf16[256,20,128]{0,2,1:T(8,128)(2,1)}, u32[]{:S(2)}) copy-start(bf16[256,20,128]{0,2,1:T(8,128)(2,1)} %copy-done.2) | copy-start | bytes 3932164
  240.6 19.1 %all-to-all-start.4 = ((f32[32,32,128]{2,1,0:T(8,128)}), f32[32,32,128]{2,1,0:T(8,128)S(1)}, u32[]{:S(2)}, u32[]{:S(2)}) async-start(f32[32,32,128]{2,1,0:T(8,128)} %copy.65), calls=%async_computation.4 | async-start | bytes 1048576 | tf_op jit(solution)/shard_map/all_to_all | solution.py:83
  246.4 76.0 %all-reduce.7.cloned.1.call-start = ((), (), s32[]{:S(2)}) async-start(), calls=%async_computation.6 | async-start | bytes 4194304 | tf_op jit(solution)/shard_map/psum | solution.py:103
  259.7 109.9 %copy-start.11 = (f32[1,32,128]{2,1,0:T(8,128)}, f32[1,32,128]{2,1,0:T(8,128)S(1)}, u32[]{:S(2)}) copy-start(f32[1,32,128]{2,1,0:T(8,128)S(1)} %bitcast_subtract_fusion.4) | copy-start | bytes 49156
  260.5 63.8 %all-to-all-start.5 = ((bf16[32,32,128]{2,1,0:T(8,128)(2,1)}), bf16[32,32,128]{2,1,0:T(8,128)(2,1)S(1)}, u32[]{:S(2)}, u32[]{:S(2)}) async-start(bf16[32,32,128]{2,1,0:T(8,128)(2,1)} %multiply_convert_fusion), calls=%async_computation.5 | async-start | bytes 524288 | tf_op jit(solution)/shard_map/all_to_all | solution.py:86
  266.1 190.2 %all-reduce.9.cloned.1.call-start = ((), (), s32[]{:S(2)}) async-start(), calls=%async_computation.7 | async-start | bytes 4194304 | tf_op jit(solution)/shard_map/psum | solution.py:103
  324.3 51.7 %copy-start.5 = (bf16[256,20,128]{2,1,0:T(8,128)(2,1)S(1)}, bf16[256,20,128]{2,1,0:T(8,128)(2,1)}, u32[]{:S(2)}) copy-start(bf16[256,20,128]{2,1,0:T(8,128)(2,1)} %fusion.22) | copy-start | bytes 3932164
  324.3 51.7 %copy-start.7 = (f32[1,1,64,32,256]{4,3,2,1,0:T(8,128)S(1)}, f32[1,1,64,32,256]{4,3,2,1,0:T(8,128)}, u32[]{:S(2)}) copy-start(f32[1,1,64,32,256]{4,3,2,1,0:T(8,128)} %param.12) | copy-start | bytes 6291460
  324.4 51.7 %copy-start.9 = (f32[1,1,64,32,256]{4,3,2,1,0:T(8,128)S(1)}, f32[1,1,64,32,256]{4,3,2,1,0:T(8,128)}, u32[]{:S(2)}) copy-start(f32[1,1,64,32,256]{4,3,2,1,0:T(8,128)} %all-reduce.7.cloned.1.call-done) | copy-start | bytes 6291460
  376.0 89.6 %copy-start.1 = (bf16[1,16,256,128]{3,2,1,0:T(8,128)(2,1)S(1)}, bf16[1,16,256,128]{3,2,1,0:T(8,128)(2,1)}, u32[]{:S(2)}) copy-start(bf16[1,16,256,128]{3,2,1,0:T(8,128)(2,1)} %param.8) | copy-start | bytes 3145732
Sparse Core Ops, SparseCore 0:
  250.2 72.1 all-reduce.6
  385.8 70.4 all-reduce.8
where the time goes:
time: 483 us; the launch traced here: 473 us
  waiting for transfers between devices  203 us (42%)
  local copies, waits for them, and re-layouts  133 us (28%)
  matrix products  47.7 us (10%)
  starting transfers between devices  35.1 us (7%)
  other arithmetic  24.7 us (5%)
  blocking collectives  15.2 us (3%)
  between operations  14.8 us (3%)
    psum x2, waiting for transfers between devices, local(): summed = lax.psum(averaged_in, 'grp')  127 us
    unnamed x150, local copies, waits for them, and re-layouts  99.9 us
    all_to_all x1, waiting for transfers between devices, local(): lax.all_to_all(send_maps, 'dev', split_axis=0, concat_axis=0, tiled=True)  46 us
    all_to_all x2, waiting for transfers between devices, local(): lax.all_to_all(outgoing, 'dev', split_axis=0, concat_axis=0, tiled=True)  24.7 us
    reshape x1, local copies, waits for them, and re-layouts, local(): jnp.dot(dict_bf, held_flat, preferred_element_type=jnp.float32)  24.1 us
    dot_general x2, matrix products, local(): lax.dot_general(lagged, held_flat, (((1,), (1,)), ((), ())), preferred_el...  18.5 us
    all_to_all x1, blocking collectives, local(): lax.all_to_all(residual_out.astype(jnp.bfloat16), 'dev', split_axis=0, co...  15.2 us
    all_to_all x2, starting transfers between devices, local(): lax.all_to_all(outgoing, 'dev', split_axis=0, concat_axis=0, tiled=True)  12.5 us
  transfers between devices with their start and end apart: 7, of which 6 were waited for; matrix products, arithmetic and copies ran while one was open for 2% of the time, Pallas kernels for 0%

commit v1 on v0

v1 whole, which is shorter than its diff:
```python
import functools

import jax
import jax.numpy as jnp
from jax import lax
from jax.experimental import pallas as pl
from jax.experimental.pallas import tpu as pltpu
from jax.sharding import PartitionSpec as P

MESH = pl.DeviceIdType.MESH
F32, BF16 = jnp.float32, jnp.bfloat16

TAPS, CHANS, FILTS, TIME = 64, 32, 256, 128
USES, DEVS, GRPS = 16, 32, 8
ZS, XS, YS = 8, 4, 4
TILE_LAGS = TAPS // GRPS
TILE = TILE_LAGS * CHANS
ROWS = TAPS * CHANS
WIDE = DEVS * TIME


def offset(step):
    place = step % ZS
    far = ZS // 2 - (place + 1) // 2
    dz = jnp.where(place % 2 == 1, far, ZS - far)
    dx = (XS - 1 - step // ZS) % XS
    return dz % ZS, dx


def kernel(
    uses_ref, owner_ref, sig_ref, maps_ref, dict_ref, dual_ref, cons_ref,
    cons_out, dual_out, res_out,
    maps_v, send_v, recv_v, dict_v, dual_v, cons_v, dictb_v, held_v, z_v, lag_v,
    sig_v, resf_v, piece_s, piece_r, res_s, res_r, sum_s, pair_r, y_s, y_r, avg_v,
    in_sem, out_sem, map_ss, map_rs, piece_ss, piece_rs, res_ss, res_rs,
    pair_ss, pair_rs, ys_ss, ys_rs, ag_ss, ag_rs, fw_ss, fw_rs,
):
    dev = lax.axis_index("dev")
    grp = lax.axis_index("grp")
    my_z, my_x = dev // XS, dev % XS
    my_y, core = grp // 2, grp % 2

    def target(step):
        dz, dx = offset(step)
        return ((my_z + dz) % ZS) * XS + (my_x + dx) % XS

    def origin(step):
        dz, dx = offset(step)
        return ((my_z + ZS - dz) % ZS) * XS + (my_x + XS - dx) % XS

    barrier = pltpu.get_barrier_semaphore()

    def greet(step, carry):
        pl.semaphore_signal(barrier, inc=1, device_id={"dev": target(step)}, device_id_type=MESH)
        return carry

    lax.fori_loop(0, DEVS - 1, greet, 0)
    for hop in range(1, YS):
        other = ((my_y + hop) % YS) * 2 + core
        pl.semaphore_signal(barrier, inc=1, device_id={"grp": other}, device_id_type=MESH)
    pl.semaphore_signal(barrier, inc=1, device_id={"grp": my_y * 2 + 1 - core}, device_id_type=MESH)

    load_maps = pltpu.make_async_copy(maps_ref.at[0], maps_v, in_sem.at[0])
    load_dict = pltpu.make_async_copy(dict_ref.at[0, 0], dict_v, in_sem.at[1])
    load_dual = pltpu.make_async_copy(dual_ref.at[0, 0], dual_v, in_sem.at[2])
    load_cons = pltpu.make_async_copy(cons_ref.at[0], cons_v, in_sem.at[3])
    load_sig = pltpu.make_async_copy(sig_ref.at[0], sig_v, in_sem.at[4])
    load_maps.start()
    load_dict.start()
    load_dual.start()
    load_cons.start()
    load_sig.start()

    slots = [owner_ref[uses_ref[0, u]] for u in range(USES)]
    load_maps.wait()
    pl.semaphore_wait(barrier, DEVS - 1 + YS)

    def block_for(d):
        at = jnp.int32(0)
        has = jnp.int32(0)
        for u in range(USES):
            hit = slots[u] == d
            at = jnp.where(hit, u, at)
            has = jnp.where(hit, 1, has)
        return maps_v[at] * has.astype(F32).astype(BF16)

    def map_copy(step, src_step, slot, to):
        return pltpu.make_async_remote_copy(
            src_ref=send_v.at[src_step],
            dst_ref=recv_v.at[slot],
            send_sem=map_ss.at[step],
            recv_sem=map_rs.at[slot],
            device_id={"dev": to},
            device_id_type=MESH,
        )

    def send_maps(step, carry):
        to = target(step)
        send_v[step] = block_for(to)
        map_copy(step, step, dev, to).start()
        return carry

    lax.fori_loop(0, DEVS - 1, send_maps, 0)
    recv_v[dev] = block_for(dev)

    load_dict.wait()

    def round_dict(tile, carry):
        rows = pl.ds(pl.multiple_of(tile * TILE, TILE), TILE)
        dictb_v[rows, :] = dict_v[pl.ds(tile * TILE_LAGS, TILE_LAGS)].reshape(TILE, FILTS).astype(BF16)
        return carry

    lax.fori_loop(0, GRPS, round_dict, 0)

    lane = lax.broadcasted_iota(jnp.int32, (CHANS, TIME), 1)

    def piece_copy(rnd, step, slot, to):
        return pltpu.make_async_remote_copy(
            src_ref=piece_s.at[rnd, step],
            dst_ref=piece_r.at[rnd, slot],
            send_sem=piece_ss.at[rnd, step],
            recv_sem=piece_rs.at[rnd, slot],
            device_id={"dev": to},
            device_id_type=MESH,
        )

    def res_copy(rnd, step, slot, to):
        return pltpu.make_async_remote_copy(
            src_ref=res_s.at[rnd],
            dst_ref=res_r.at[rnd, slot],
            send_sem=res_ss.at[rnd, step],
            recv_sem=res_rs.at[rnd, slot],
            device_id={"dev": to},
            device_id_type=MESH,
        )

    def spread(rnd):
        def pair(index, carry):
            first, second = 2 * index, 2 * index + 1
            from_first, from_second = origin(first), origin(second)
            if rnd == 0:
                map_copy(first, first, from_first, from_first).wait_recv()

                @pl.when(second < DEVS - 1)
                def _():
                    map_copy(second, second, from_second, from_second).wait_recv()

            one, two = recv_v[from_first], recv_v[from_second]
            if rnd == 0:
                held_v[pl.ds(pl.multiple_of(first * TIME, TIME), TIME), :] = one.T
                held_v[pl.ds(pl.multiple_of(second * TIME, TIME), TIME), :] = two.T
            block = jnp.concatenate([one, two], axis=1)
            total = [jnp.zeros((CHANS, TIME), F32), jnp.zeros((CHANS, TIME), F32)]
            for tile in range(GRPS):
                product = jnp.dot(
                    dictb_v[tile * TILE : (tile + 1) * TILE, :], block, preferred_element_type=F32
                )
                for near in range(TILE_LAGS):
                    lag = tile * TILE_LAGS + near
                    for half in range(2):
                        part = product[near * CHANS : (near + 1) * CHANS, half * TIME : (half + 1) * TIME]
                        if lag > 0:
                            part = jnp.where(lane >= lag, pltpu.roll(part, lag, 1), 0.0)
                        total[half] = total[half] + part
            piece_s[rnd, first] = total[0].astype(BF16)
            piece_s[rnd, second] = total[1].astype(BF16)
            piece_copy(rnd, first, dev, from_first).start()

            @pl.when(second < DEVS - 1)
            def _():
                piece_copy(rnd, second, dev, from_second).start()

            return carry

        lax.fori_loop(0, DEVS // 2, pair, 0)

    def residual(rnd):
        def add(step, total):
            slot = origin(step)
            piece_copy(rnd, step, slot, slot).wait_recv()
            return total + piece_r[rnd, slot].astype(F32)

        recon = lax.fori_loop(0, DEVS - 1, add, piece_s[rnd, DEVS - 1].astype(F32))
        left = sig_v[...] - recon
        res_s[rnd] = left.astype(BF16)

        def post(step, carry):
            res_copy(rnd, step, dev, target(step)).start()
            return carry

        lax.fori_loop(0, DEVS - 1, post, 0)
        return left

    def lagged(rnd):
        def window(back, carry):
            step = DEVS - 1 - back
            slot = origin(step)

            @pl.when(back > 0)
            def _():
                res_copy(rnd, step, slot, slot).wait_recv()
                resf_v[step] = res_r[rnd, slot].astype(F32)

            @pl.when(back == 0)
            def _():
                resf_v[step] = res_s[rnd].astype(F32)

            left = resf_v[step]
            columns = pl.ds(pl.multiple_of(step * TIME, TIME), TIME)
            for lag in range(TAPS):
                part = left
                if lag > 0:
                    part = jnp.where(lane < TIME - lag, pltpu.roll(left, TIME - lag, 1), 0.0)
                lag_v[lag * CHANS : (lag + 1) * CHANS, columns] = part.astype(BF16)
            return carry

        lax.fori_loop(0, DEVS, window, 0)

    def pair_copy(rnd, y):
        return pltpu.make_async_remote_copy(
            src_ref=sum_s.at[rnd, 2 * y + 1 - core],
            dst_ref=pair_r.at[rnd, y],
            send_sem=pair_ss.at[rnd, y],
            recv_sem=pair_rs.at[rnd, y],
            device_id={"grp": my_y * 2 + 1 - core},
            device_id_type=MESH,
        )

    def y_copy(rnd, y, slot):
        return pltpu.make_async_remote_copy(
            src_ref=y_s.at[rnd, y],
            dst_ref=y_r.at[rnd, slot],
            send_sem=ys_ss.at[rnd, y],
            recv_sem=ys_rs.at[rnd, slot],
            device_id={"grp": y * 2 + core},
            device_id_type=MESH,
        )

    def gather_copy(rnd, y, slot):
        return pltpu.make_async_remote_copy(
            src_ref=avg_v.at[rnd, slot * 2 + core],
            dst_ref=avg_v.at[rnd, slot * 2 + core],
            send_sem=ag_ss.at[rnd, y],
            recv_sem=ag_rs.at[rnd, slot],
            device_id={"grp": y * 2 + core},
            device_id_type=MESH,
        )

    def forward_copy(rnd, y, whose):
        return pltpu.make_async_remote_copy(
            src_ref=avg_v.at[rnd, y * 2 + whose],
            dst_ref=avg_v.at[rnd, y * 2 + whose],
            send_sem=fw_ss.at[rnd, y],
            recv_sem=fw_rs.at[rnd, y],
            device_id={"grp": my_y * 2 + 1 - core},
            device_id_type=MESH,
        )

    def gradient(rnd):
        def tile_step(tile, carry):
            rows = pl.ds(pl.multiple_of(tile * TILE, TILE), TILE)
            lags = pl.ds(tile * TILE_LAGS, TILE_LAGS)
            grad = jnp.dot(lag_v[rows, :], held_v[...], preferred_element_type=F32)
            grad = grad.reshape(TILE_LAGS, CHANS, FILTS)
            if rnd == 0:
                dual = dual_v[lags]
                new_dict = (dict_v[lags] + 4.0 * grad + (cons_v[lags] - dual)) * 0.5
                dict_v[lags] = new_dict
                dictb_v[rows, :] = new_dict.reshape(TILE, FILTS).astype(BF16)
                share = new_dict + dual
            else:
                share = z_v[lags] + 2.0 * grad
                z_v[lags] = share
            sum_s[rnd, tile] = share.reshape(TILE, FILTS).astype(BF16)

            @pl.when(tile % 2 != core)
            def _():
                pair_copy(rnd, tile // 2).start()

            return carry

        lax.fori_loop(0, GRPS, tile_step, 0)

    def group_pairs(rnd):
        for hop in (2, 1, 3, 0):
            y = (my_y + hop) % YS
            pair_copy(rnd, y).wait_recv()
            both = sum_s[rnd, 2 * y + core].astype(F32) + pair_r[rnd, y].astype(F32)
            y_s[rnd, y] = both.astype(BF16)
            if hop:
                y_copy(rnd, y, my_y).start()

    def group_mean(rnd):
        total = y_s[rnd, my_y].astype(F32)
        for hop in (1, 3, 2):
            y = (my_y + hop) % YS
            y_copy(rnd, y, y).wait_recv()
            total = total + y_r[rnd, y].astype(F32)
        avg_v[rnd, grp] = (total * (1.0 / GRPS)).astype(BF16)
        for hop in (2, 1, 3):
            gather_copy(rnd, (my_y + hop) % YS, my_y).start()
        forward_copy(rnd, my_y, core).start()

    def group_forward(rnd):
        for hop in (1, 3, 2):
            y = (my_y + hop) % YS
            gather_copy(rnd, y, y).wait_recv()
            forward_copy(rnd, y, core).start()

    def group_norm(rnd):
        for y in range(YS):
            forward_copy(rnd, y, 1 - core).wait_recv()

        def squares(tile, total):
            part = avg_v[rnd, tile].astype(F32)
            return total + jnp.sum((part * part).reshape(TILE // 8, 8, FILTS), axis=0)

        total = lax.fori_loop(0, GRPS, squares, jnp.zeros((8, FILTS), F32))
        norm = jnp.sqrt(jnp.sum(total, axis=0, keepdims=True))
        return 1.0 / jnp.maximum(1.0, norm * (1.0 / ROWS**0.5))

    spread(0)
    load_sig.wait()
    residual(0)
    load_dual.wait()
    load_cons.wait()
    lagged(0)
    gradient(0)
    group_pairs(0)

    spread(1)
    group_mean(0)
    left = residual(1)
    resf_v[0] = left
    store_res = pltpu.make_async_copy(resf_v.at[0], res_out.at[0], out_sem.at[2])
    store_res.start()
    store_res.wait()
    group_forward(0)
    scale = group_norm(0)

    def carry_over(tile, carry):
        lags = pl.ds(tile * TILE_LAGS, TILE_LAGS)
        cons = (avg_v[0, tile].astype(F32) * scale).reshape(TILE_LAGS, CHANS, FILTS)
        new_dict = dict_v[lags]
        dual = dual_v[lags] + new_dict - cons
        z_v[lags] = (new_dict + (cons - dual)) * 0.5 + dual
        return carry

    lax.fori_loop(0, GRPS, carry_over, 0)
    lagged(1)
    gradient(1)
    group_pairs(1)
    group_mean(1)
    group_forward(1)
    scale = group_norm(1)

    def out_copies(tile):
        lags = pl.ds(tile * TILE_LAGS, TILE_LAGS)
        return (
            pltpu.make_async_copy(cons_v.at[lags], cons_out.at[0, lags], out_sem.at[0]),
            pltpu.make_async_copy(dual_v.at[lags], dual_out.at[0, 0, lags], out_sem.at[1]),
        )

    def finish(tile, carry):
        lags = pl.ds(tile * TILE_LAGS, TILE_LAGS)
        cons = (avg_v[1, tile].astype(F32) * scale).reshape(TILE_LAGS, CHANS, FILTS)
        cons_v[lags] = cons
        dual_v[lags] = z_v[lags] - cons
        return carry

    lax.fori_loop(0, GRPS, finish, 0)
    store_cons = pltpu.make_async_copy(cons_v, cons_out.at[0], out_sem.at[0])
    store_dual = pltpu.make_async_copy(dual_v, dual_out.at[0, 0], out_sem.at[1])
    store_cons.start()
    store_dual.start()

    def sent(step, carry):
        map_copy(step, step, dev, dev).wait_send()
        for rnd in range(2):
            piece_copy(rnd, step, dev, dev).wait_send()
            res_copy(rnd, step, dev, dev).wait_send()
        return carry

    lax.fori_loop(0, DEVS - 1, sent, 0)
    for rnd in range(2):
        for y in range(YS):
            pair_copy(rnd, y).wait_send()
            forward_copy(rnd, y, core).wait_send()
        for hop in range(1, YS):
            y = (my_y + hop) % YS
            y_copy(rnd, y, my_y).wait_send()
            gather_copy(rnd, y, my_y).wait_send()
    store_cons.wait()
    store_dual.wait()


def local(signals, maps, uses, owner, local_dict, duals, consensus):
    vmem = pltpu.VMEM
    dma = pltpu.SemaphoreType.DMA
    big = (TAPS, CHANS, FILTS)
    anywhere = pl.BlockSpec(memory_space=pl.ANY)
    return pl.pallas_call(
        kernel,
        out_shape=(
            jax.ShapeDtypeStruct(consensus.shape, F32),
            jax.ShapeDtypeStruct(duals.shape, F32),
            jax.ShapeDtypeStruct(signals.shape, F32),
        ),
        in_specs=[pl.BlockSpec(memory_space=pltpu.SMEM)] * 2 + [anywhere] * 5,
        out_specs=(anywhere,) * 3,
        scratch_shapes=[
            vmem((USES, FILTS, TIME), BF16),
            vmem((DEVS, FILTS, TIME), BF16),
            vmem((DEVS, FILTS, TIME), BF16),
            vmem(big, F32),
            vmem(big, F32),
            vmem(big, F32),
            vmem((ROWS, FILTS), BF16),
            vmem((WIDE, FILTS), BF16),
            vmem(big, F32),
            vmem((ROWS, WIDE), BF16),
            vmem((CHANS, TIME), F32),
            vmem((DEVS, CHANS, TIME), F32),
            vmem((2, DEVS, CHANS, TIME), BF16),
            vmem((2, DEVS, CHANS, TIME), BF16),
            vmem((2, CHANS, TIME), BF16),
            vmem((2, DEVS, CHANS, TIME), BF16),
            vmem((2, GRPS, TILE, FILTS), BF16),
            vmem((2, YS, TILE, FILTS), BF16),
            vmem((2, YS, TILE, FILTS), BF16),
            vmem((2, YS, TILE, FILTS), BF16),
            vmem((2, GRPS, TILE, FILTS), BF16),
            dma((5,)),
            dma((3,)),
            dma((DEVS,)),
            dma((DEVS,)),
            dma((2, DEVS)),
            dma((2, DEVS)),
            dma((2, DEVS)),
            dma((2, DEVS)),
        ]
        + [dma((2, YS))] * 8,
        compiler_params=pltpu.CompilerParams(
            collective_id=0, has_side_effects=True, vmem_limit_bytes=56 * 1024 * 1024
        ),
        cost_estimate=pl.CostEstimate(flops=17_000_000_000, bytes_accessed=12_000_000, transcendentals=0),
    )(uses, owner, signals, maps, local_dict, duals, consensus)


def solution(mesh):
    placed = (
        P(("grp", "dev"), None, None),
        P(("grp", "dev"), None, None, None),
        P(("grp", "dev"), None),
        P(),
        P("grp", "dev", None, None, None),
        P("grp", "dev", None, None, None),
        P("dev", None, None, None),
    )
    return jax.shard_map(
        local,
        mesh=mesh,
        in_specs=placed,
        out_specs=(
            P("dev", None, None, None),
            P("grp", "dev", None, None, None),
            P(("grp", "dev"), None, None),
        ),
        check_vma=False,
    )
```

time: 483 us -> 156 us (0.32); the launches traced: 473 us -> 153 us
  waiting for transfers between devices: 203 us -> 0 us
  Pallas kernels: 0 us -> 147 us
  local copies, waits for them, and re-layouts: 133 us -> 5.24 us
  matrix products: 47.7 us -> 0 us
  starting transfers between devices: 35.1 us -> 0 us
  other arithmetic: 24.7 us -> 0 us
  blocking collectives: 15.2 us -> 0 us
  between operations: 14.8 us -> 0.65 us
    pallas_call x0 -> x1, Pallas kernels: none -> 147 us  [local(): pl.pallas_call(kernel, out_shape=(jax.ShapeDtypeStruct(consensus.shape, F...]
    psum x2 -> x0, waiting for transfers between devices: 127 us -> none  [local(): summed = lax.psum(averaged_in, 'grp')]
    unnamed x150 -> x7, local copies, waits for them, and re-layouts: 99.9 us -> 5.24 us
    all_to_all x5 -> x0, waiting for transfers between devices: 76 us -> none  [the longest x1 46 us: local(): lax.all_to_all(send_maps, 'dev', split_axis=0, concat_axis=0, tiled=True)]
    dot_general x10 -> x0, matrix products: 47.7 us -> none  [the longest x2 18.5 us: local(): lax.dot_general(lagged, held_flat, (((1,), (1,)), ((), ())), preferred_el...]
    all_to_all x5 -> x0, starting transfers between devices: 34.8 us -> none  [the longest x2 12.5 us: local(): lax.all_to_all(outgoing, 'dev', split_axis=0, concat_axis=0, tiled=True)]
    reshape x1 -> x0, local copies, waits for them, and re-layouts: 24.1 us -> none  [local(): jnp.dot(dict_bf, held_flat, preferred_element_type=jnp.float32)]
    all_to_all x1 -> x0, blocking collectives: 15.2 us -> none  [local(): lax.all_to_all(residual_out.astype(jnp.bfloat16), 'dev', split_axis=0, co...]
  transfers between devices with their start and end apart: 7 -> 0, of which waited for: 6 -> 0; matrix products, arithmetic and copies ran while one was open for 2% -> 0% of each run, Pallas kernels for 0% -> 0%
where the time goes in v1:
time: 156 us; the launch traced here: 153 us
  Pallas kernels  147 us (94%)
  local copies, waits for them, and re-layouts  5.24 us (3%)
    pallas_call x1, Pallas kernels, local(): pl.pallas_call(kernel, out_shape=(jax.ShapeDtypeStruct(consensus.shape, F...  147 us
    unnamed x7, local copies, waits for them, and re-layouts  5.24 us

profile of v1, /device:TPU:2, one launch (start us, length us, event | category | flops | bytes accessed | tf_op | source)
XLA Modules:
  0.0 153.2 jit_solution(14671999499197808049)
XLA Ops:
  0.6 147.4 %shard_map.94 = (f32[1,64,32,256]{3,2,1,0:T(8,128)}, f32[1,1,64,32,256]{4,3,2,1,0:T(8,128)}, f32[1,32,128]{2,1,0:T(8,128)}) custom-call(s32[1,16]{1,0:T(1,128)} %uses_ref.1, s32[32]{0:T(128)} %owner_ref.1, f32[1,32,128]{2,1,0:T(8,128)} %sig_ref.1, bf16[1,16,256,128]{3,2,1,0:T(8,128)(2,1)} %maps_ref.1, f32[1,1,64,32,256]{4,3,2,1,0:T(8,128)} %dict_ref.1, ...), custom_call_target="tpu_custom_call" | custom-call | flops 16999999488 | bytes 12000000 | tf_op jit(solution)/shard_map/pallas_call | solution.py:402
  148.0 0.0 copy-start
  148.0 3.3 %copy.13 = f32[1,64,32,256]{3,2,1,0:T(8,128)} copy(f32[1,64,32,256]{3,2,1,0:T(8,128)} %get-tuple-element.6) | data formatting | bytes 4194304
  151.3 0.0 copy-done
  151.3 0.0 copy-start.1
  151.3 1.3 copy.14
  152.6 0.0 copy-done.1
  152.6 0.6 copy.15
Async XLA Ops:
  148.0 3.3 %copy-start = (f32[1,1,64,32,256]{4,3,2,1,0:T(8,128)S(1)}, f32[1,1,64,32,256]{4,3,2,1,0:T(8,128)}, u32[]{:S(2)}) copy-start(f32[1,1,64,32,256]{4,3,2,1,0:T(8,128)} %get-tuple-element.7) | copy-start | bytes 6291460
  151.3 1.3 copy-start.1

commit v2 on v1

v2 whole, which is shorter than its diff:
```python
import jax
import jax.numpy as jnp
from jax import lax
from jax.experimental import pallas as pl
from jax.experimental.pallas import tpu as pltpu
from jax.sharding import PartitionSpec as P

MESH = pl.DeviceIdType.MESH
F32, BF16 = jnp.float32, jnp.bfloat16

TAPS, CHANS, FILTS, TIME = 64, 32, 256, 128
USES, DEVS, GRPS = 16, 32, 8
ZS, XS, YS = 8, 4, 4
FINE = 8
COARSE = TAPS // FINE
TILE = COARSE * CHANS
ROWS = TAPS * CHANS
BATCH = TIME // CHANS


def offset(step):
    place = step + XS
    far = ZS // 2 - place // ZS
    dz = jnp.where(place % 2 == 1, far, ZS - far) % ZS
    dx = jnp.where(far % (ZS // 2) == 0, DEVS + XS - 1 - place, place // 2) % XS
    return dz, dx


def fixed_offset(step):
    place = step + XS
    far = ZS // 2 - place // ZS
    dz = (far if place % 2 == 1 else ZS - far) % ZS
    dx = (DEVS + XS - 1 - place if far % (ZS // 2) == 0 else place // 2) % XS
    return dz, dx


def later(values, rows):
    if rows == 0:
        return values
    return jnp.concatenate([jnp.zeros((rows, values.shape[1]), values.dtype), values[:-rows]], axis=0)


def kernel(
    uses_ref, owner_ref, sig_ref, maps_ref, dict_ref, dual_ref, cons_ref,
    cons_out, dual_out, res_out,
    maps_v, send_v, recv_v, dict_v, dual_v, cons_v, dictt_v, stage_v, mapst_v, lag_v, z_v,
    sig_v, piece_s, piece_r, res_s, res_r, left_v,
    sum_f, pair_f, sum_b, pair_b, y_s, y_r, avg_v, change_v, rest_v,
    in_sem, map_ss, map_rs, piece_ss, piece_rs, res_ss, res_rs,
    pair_ss, pair_rs, ys_ss, ys_rs, ag_ss, ag_rs, fw_ss, fw_rs,
):
    dev = lax.axis_index("dev")
    grp = lax.axis_index("grp")
    my_z, my_x = dev // XS, dev % XS
    my_y, core = grp // 2, grp % 2

    rows_of = [((my_z + dz) % ZS) * XS for dz in range(ZS)]
    columns_of = [(my_x + dx) % XS for dx in range(XS)]

    def target(step):
        dz, dx = fixed_offset(step)
        return rows_of[dz] + columns_of[dx]

    def origin(step):
        dz, dx = offset(step)
        return ((my_z + ZS - dz) % ZS) * XS + (my_x + XS - dx) % XS

    barrier = pltpu.get_barrier_semaphore()

    for step in range(DEVS - 1):
        pl.semaphore_signal(barrier, inc=1, device_id={"dev": target(step)}, device_id_type=MESH)
    for hop in range(1, YS):
        other = ((my_y + hop) % YS) * 2 + core
        pl.semaphore_signal(barrier, inc=1, device_id={"grp": other}, device_id_type=MESH)
    pl.semaphore_signal(barrier, inc=1, device_id={"grp": my_y * 2 + 1 - core}, device_id_type=MESH)

    load_maps = pltpu.make_async_copy(maps_ref.at[0], maps_v, in_sem.at[0])
    load_dict = pltpu.make_async_copy(dict_ref, dict_v, in_sem.at[1])
    load_dual = pltpu.make_async_copy(dual_ref, dual_v, in_sem.at[2])
    load_cons = pltpu.make_async_copy(cons_ref, cons_v, in_sem.at[3])
    load_sig = pltpu.make_async_copy(sig_ref.at[0], sig_v, in_sem.at[4])
    load_maps.start()
    load_dict.start()
    load_dual.start()
    load_cons.start()
    load_sig.start()

    slots = [owner_ref[uses_ref[0, u]] for u in range(USES)]
    load_maps.wait()

    def block_for(d):
        at = jnp.int32(0)
        has = jnp.int32(0)
        for u in range(USES):
            hit = slots[u] == d
            at = jnp.where(hit, u, at)
            has = jnp.where(hit, 1, has)
        return maps_v[at] * has.astype(F32).astype(BF16)

    def map_copy(step, to):
        return pltpu.make_async_remote_copy(
            src_ref=send_v.at[step],
            dst_ref=recv_v.at[step],
            send_sem=map_ss.at[step],
            recv_sem=map_rs.at[step],
            device_id={"dev": to},
            device_id_type=MESH,
        )

    pl.semaphore_wait(barrier, DEVS - 1 + YS)
    for step in range(DEVS - 1):
        send_v[step] = block_for(target(step))
        map_copy(step, target(step)).start()
    recv_v[DEVS - 1] = block_for(dev)

    load_dict.wait()

    def turned(tile):
        return tile.reshape(TILE, FILTS).astype(BF16).T

    def turn_dict(tile, carry):
        dictt_v[pl.ds(pl.multiple_of(tile * FILTS, FILTS), FILTS), :] = turned(dict_v[:, tile])
        return carry

    lax.fori_loop(0, FINE, turn_dict, 0)
    for place in range(BATCH):
        stage_v[place, :FINE, :] = jnp.zeros((FINE, FILTS), F32)

    lane_t = lax.broadcasted_iota(jnp.int32, (CHANS, TIME), 1)
    lane_part = lax.broadcasted_iota(jnp.int32, (TIME, TIME), 1) // CHANS

    def piece_copy(rnd, step, to):
        return pltpu.make_async_remote_copy(
            src_ref=piece_s.at[rnd, step],
            dst_ref=piece_r.at[rnd, step],
            send_sem=piece_ss.at[rnd, step],
            recv_sem=piece_rs.at[rnd, step],
            device_id={"dev": to},
            device_id_type=MESH,
        )

    def res_copy(rnd, step, to):
        return pltpu.make_async_remote_copy(
            src_ref=res_s.at[rnd],
            dst_ref=res_r.at[rnd, step],
            send_sem=res_ss.at[rnd, step],
            recv_sem=res_rs.at[rnd, step],
            device_id={"dev": to},
            device_id_type=MESH,
        )

    def fold(product):
        half = product[:, :TIME] + later(product[:, TIME:], BATCH * FINE)
        mixed = half
        for part in range(1, BATCH):
            mixed = jnp.where(lane_part == part, later(half, part * FINE), mixed)
        mixed = mixed + pltpu.roll(mixed, 2 * CHANS, 1)
        return mixed + pltpu.roll(mixed, CHANS, 1)

    def spread(rnd, low, high):
        def batch(index, carry):
            first = index * BATCH
            if rnd == 0:
                for place in range(BATCH):
                    step = first + place
                    if place == BATCH - 1:

                        @pl.when(step < DEVS - 1)
                        def _():
                            map_copy(step, origin(step)).wait_recv()

                    else:
                        map_copy(step, origin(step)).wait_recv()
                for place in range(BATCH):
                    step = first + place
                    stage_v[place, FINE:, :] = recv_v[step].T.astype(F32)
                    for fine in range(FINE):
                        mapst_v[step, :, fine * FILTS : (fine + 1) * FILTS] = stage_v[
                            place, FINE - fine : FINE - fine + TIME, :
                        ].astype(BF16)
            held = mapst_v[pl.ds(first, BATCH)].reshape(BATCH * TIME, FINE * FILTS)
            product = jnp.dot(held, dictt_v[...], preferred_element_type=F32)
            gathered = fold(product[:TIME])
            for place in range(1, BATCH):
                one = fold(product[place * TIME : (place + 1) * TIME])
                gathered = jnp.where(lane_part == place, one, gathered)
            pieces = gathered.T.astype(BF16)
            for place in range(BATCH):
                piece_s[rnd, first + place] = pieces[place * CHANS : (place + 1) * CHANS]
            for place in range(BATCH):
                step = first + place
                if place == BATCH - 1:

                    @pl.when(step < DEVS - 1)
                    def _():
                        piece_copy(rnd, step, origin(step)).start()

                else:
                    piece_copy(rnd, step, origin(step)).start()
            return carry

        lax.fori_loop(low, high, batch, 0)

    def residual(rnd):
        for step in range(DEVS - 1):
            piece_copy(rnd, step, target(step)).wait_recv()
        parts = [piece_r[rnd, step].astype(F32) for step in range(DEVS - 1)]
        parts.append(piece_s[rnd, DEVS - 1].astype(F32))
        while len(parts) > 1:
            parts = [one + two for one, two in zip(parts[::2], parts[1::2], strict=True)]
        recon = parts[0]
        left = sig_v[...] - recon
        res_s[rnd] = left.astype(BF16)
        left_v[DEVS - 1] = left.astype(BF16).astype(F32)

        for step in range(DEVS - 1):
            res_copy(rnd, step, target(step)).start()
        return left

    def lagged(rnd):
        for step in range(DEVS - 1):
            res_copy(rnd, step, target(step)).wait_recv()
            left_v[step] = res_r[rnd, step].astype(F32)

        def some(index, carry):
            for place in range(BATCH):
                step = index * BATCH + place
                left = left_v[step]
                columns = pl.ds(pl.multiple_of(step * TIME, TIME), TIME)
                for coarse in range(COARSE):
                    lag = coarse * FINE
                    part = left
                    if lag > 0:
                        part = jnp.where(lane_t < TIME - lag, pltpu.roll(left, TIME - lag, 1), 0.0)
                    lag_v[coarse * CHANS : (coarse + 1) * CHANS, columns] = part.astype(BF16)
            return carry

        lax.fori_loop(0, DEVS // BATCH, some, 0)

    def pair_copy(rnd, y):
        sums, pairs = ((sum_f, pair_f), (sum_b, pair_b))[rnd]
        return pltpu.make_async_remote_copy(
            src_ref=sums.at[2 * y + 1 - core],
            dst_ref=pairs.at[y],
            send_sem=pair_ss.at[rnd, y],
            recv_sem=pair_rs.at[rnd, y],
            device_id={"grp": my_y * 2 + 1 - core},
            device_id_type=MESH,
        )

    def y_copy(rnd, y, slot):
        return pltpu.make_async_remote_copy(
            src_ref=y_s.at[rnd, y],
            dst_ref=y_r.at[rnd, slot],
            send_sem=ys_ss.at[rnd, y],
            recv_sem=ys_rs.at[rnd, slot],
            device_id={"grp": y * 2 + core},
            device_id_type=MESH,
        )

    means = (avg_v, change_v, rest_v)

    def gather_copy(kind, y, slot):
        where = means[kind].at[slot * 2 + core]
        return pltpu.make_async_remote_copy(
            src_ref=where,
            dst_ref=where,
            send_sem=ag_ss.at[kind, y],
            recv_sem=ag_rs.at[kind, slot],
            device_id={"grp": y * 2 + core},
            device_id_type=MESH,
        )

    def forward_copy(kind, y, whose):
        where = means[kind].at[y * 2 + whose]
        return pltpu.make_async_remote_copy(
            src_ref=where,
            dst_ref=where,
            send_sem=fw_ss.at[kind, y],
            recv_sem=fw_rs.at[kind, y],
            device_id={"grp": my_y * 2 + 1 - core},
            device_id_type=MESH,
        )

    def gradient(rnd):
        sums, pairs = ((sum_f, pair_f), (sum_b, pair_b))[rnd]

        def one_tile(tile):
            wide = pl.ds(pl.multiple_of(tile * FILTS, FILTS), FILTS)
            held = mapst_v[:, :, wide].reshape(DEVS * TIME, FILTS)
            grad = jnp.dot(lag_v[...], held, preferred_element_type=F32)
            if rnd == 0:
                grad = grad.reshape(COARSE, CHANS, FILTS)
                dual = dual_v[:, tile]
                new_dict = (dict_v[:, tile] + 4.0 * grad + (cons_v[:, tile] - dual)) * 0.5
                dict_v[:, tile] = new_dict
                dictt_v[wide, :] = turned(new_dict)
                sum_f[tile] = (new_dict + dual).reshape(TILE, FILTS)
            else:
                both = z_v[tile] + 2.0 * grad
                z_v[tile] = both
                sum_b[tile] = (both - sum_f[tile]).astype(BF16)

        def add_pair(y):
            pair_copy(rnd, y).wait_recv()
            both = sums[2 * y + core].astype(F32) + pairs[y].astype(F32)
            y_s[rnd, y] = both.astype(BF16)

        def two_tiles(y):
            one_tile(2 * y + 1 - core)
            pair_copy(rnd, y).start()
            one_tile(2 * y + core)
            add_pair(y)

        def away(turn, carry):
            y = (my_y + 1 + turn) % YS
            two_tiles(y)
            y_copy(rnd, y, my_y).start()
            return carry

        lax.fori_loop(0, YS - 1, away, 0)
        two_tiles(my_y)

    def group_mean(rnd):
        total = y_s[rnd, my_y].astype(F32)
        for hop in (1, 3, 2):
            y = (my_y + hop) % YS
            y_copy(rnd, y, y).wait_recv()
            total = total + y_r[rnd, y].astype(F32)
        total = total * (1.0 / GRPS)
        kinds = (0, 2) if rnd == 0 else (1,)
        for kind in kinds:
            short = total.astype(BF16)
            means[kind][grp] = short
            total = total - short.astype(F32)
            for hop in (2, 1, 3):
                gather_copy(kind, (my_y + hop) % YS, my_y).start()
            forward_copy(kind, my_y, core).start()

    def group_forward(kind):
        for hop in (1, 3, 2):
            y = (my_y + hop) % YS
            gather_copy(kind, y, y).wait_recv()
            forward_copy(kind, y, core).start()

    def group_close(kind):
        for y in range(YS):
            forward_copy(kind, y, 1 - core).wait_recv()

    def mean_of(rnd, tile):
        mean = avg_v[tile].astype(F32)
        if rnd == 1:
            mean = mean + rest_v[tile].astype(F32) + change_v[tile].astype(F32)
        return mean

    def scale_of(rnd):
        def squares(tile, total):
            part = mean_of(rnd, tile)
            return total + jnp.sum((part * part).reshape(TILE // 8, 8, FILTS), axis=0)

        total = lax.fori_loop(0, FINE, squares, jnp.zeros((8, FILTS), F32))
        norm = jnp.sqrt(jnp.sum(total, axis=0, keepdims=True))
        return 1.0 / jnp.maximum(1.0, norm * (1.0 / ROWS**0.5))

    batches = DEVS // BATCH

    spread(0, 0, batches)
    load_sig.wait()
    residual(0)
    load_dual.wait()
    load_cons.wait()
    lagged(0)
    gradient(0)

    spread(1, 0, batches // 2)
    group_mean(0)
    spread(1, batches // 2, batches)
    res_out[0] = residual(1)
    group_forward(0)
    group_close(0)
    scale = scale_of(0)

    def carry_over(tile, carry):
        cons = (mean_of(0, tile) * scale).reshape(COARSE, CHANS, FILTS)
        new_dict = dict_v[:, tile]
        dual = dual_v[:, tile] + new_dict - cons
        z_v[tile] = ((new_dict + (cons - dual)) * 0.5 + dual).reshape(TILE, FILTS)
        return carry

    lax.fori_loop(0, FINE, carry_over, 0)
    lagged(1)
    gradient(1)
    group_forward(2)
    group_mean(1)
    group_close(2)
    group_forward(1)
    group_close(1)
    scale_end = scale_of(1)

    def finish(tile, carry):
        cons = mean_of(1, tile) * scale_end
        cons_out[:, tile] = cons.reshape(COARSE, CHANS, FILTS)
        dual_out[:, tile] = (z_v[tile] - cons).reshape(COARSE, CHANS, FILTS)
        return carry

    lax.fori_loop(0, FINE, finish, 0)

    for step in range(DEVS - 1):
        map_copy(step, target(step)).wait_send()
        for rnd in range(2):
            piece_copy(rnd, step, target(step)).wait_send()
            res_copy(rnd, step, target(step)).wait_send()
    for rnd in range(2):
        for y in range(YS):
            pair_copy(rnd, y).wait_send()
        for hop in range(1, YS):
            y_copy(rnd, (my_y + hop) % YS, my_y).wait_send()
    for kind in range(3):
        for y in range(YS):
            forward_copy(kind, y, core).wait_send()
        for hop in range(1, YS):
            gather_copy(kind, (my_y + hop) % YS, my_y).wait_send()


def local(signals, maps, uses, owner, local_dict, duals, consensus):
    vmem = pltpu.VMEM
    dma = pltpu.SemaphoreType.DMA
    split = (COARSE, FINE, CHANS, FILTS)
    tiles = (FINE, TILE, FILTS)
    quarter = (YS, TILE, FILTS)
    cons_new, dual_new, left = pl.pallas_call(
        kernel,
        out_shape=(
            jax.ShapeDtypeStruct(split, F32),
            jax.ShapeDtypeStruct(split, F32),
            jax.ShapeDtypeStruct(signals.shape, F32),
        ),
        in_specs=[pl.BlockSpec(memory_space=pltpu.SMEM)] * 2 + [pl.BlockSpec(memory_space=pltpu.HBM)] * 5,
        out_specs=(pl.BlockSpec(memory_space=pltpu.VMEM),) * 3,
        scratch_shapes=[
            vmem((USES, FILTS, TIME), BF16),
            vmem((DEVS, FILTS, TIME), BF16),
            vmem((DEVS, FILTS, TIME), BF16),
            vmem(split, F32),
            vmem(split, F32),
            vmem(split, F32),
            vmem((FINE * FILTS, TILE), BF16),
            vmem((BATCH, FINE + TIME, FILTS), F32),
            vmem((DEVS, TIME, FINE * FILTS), BF16),
            vmem((TILE, DEVS * TIME), BF16),
            vmem(tiles, F32),
            vmem((CHANS, TIME), F32),
            vmem((2, DEVS, CHANS, TIME), BF16),
            vmem((2, DEVS, CHANS, TIME), BF16),
            vmem((2, CHANS, TIME), BF16),
            vmem((2, DEVS, CHANS, TIME), BF16),
            vmem((DEVS, CHANS, TIME), F32),
            vmem(tiles, F32),
            vmem(quarter, F32),
            vmem(tiles, BF16),
            vmem(quarter, BF16),
            vmem((2,) + quarter, BF16),
            vmem((2,) + quarter, BF16),
            vmem(tiles, BF16),
            vmem(tiles, BF16),
            vmem(tiles, BF16),
            dma((5,)),
            dma((DEVS,)),
            dma((DEVS,)),
            dma((2, DEVS)),
            dma((2, DEVS)),
            dma((2, DEVS)),
            dma((2, DEVS)),
        ]
        + [dma((2, YS))] * 4
        + [dma((3, YS))] * 4,
        compiler_params=pltpu.CompilerParams(
            collective_id=0, has_side_effects=True, vmem_limit_bytes=48 * 1024 * 1024
        ),
        cost_estimate=pl.CostEstimate(flops=17_000_000_000, bytes_accessed=12_000_000, transcendentals=0),
    )(uses, owner, signals, maps, local_dict.reshape(split), duals.reshape(split), consensus.reshape(split))
    return cons_new.reshape(consensus.shape), dual_new.reshape(duals.shape), left


def solution(mesh):
    placed = (
        P(("grp", "dev"), None, None),
        P(("grp", "dev"), None, None, None),
        P(("grp", "dev"), None),
        P(),
        P("grp", "dev", None, None, None),
        P("grp", "dev", None, None, None),
        P("dev", None, None, None),
    )
    return jax.shard_map(
        local,
        mesh=mesh,
        in_specs=placed,
        out_specs=(
            P("dev", None, None, None),
            P("grp", "dev", None, None, None),
            P(("grp", "dev"), None, None),
        ),
        check_vma=False,
    )
```

time: 156 us -> 145 us (0.929)
  Pallas kernels: 147 us -> 135 us
    pallas_call x1, Pallas kernels: 147 us -> 135 us  [local(): pl.pallas_call(kernel, out_shape=(jax.ShapeDtypeStruct(split, F32), jax.S...]
    unnamed x7 -> x11, local copies, waits for them, and re-layouts: 5.24 us -> 6.49 us
where the time goes in v2:
time: 145 us; the launch traced here: 142 us
  Pallas kernels  135 us (93%)
  local copies, waits for them, and re-layouts  6.49 us (4%)
    pallas_call x1, Pallas kernels, local(): pl.pallas_call(kernel, out_shape=(jax.ShapeDtypeStruct(split, F32), jax.S...  135 us
    unnamed x11, local copies, waits for them, and re-layouts  6.49 us

profile of v2, /device:TPU:2, one launch (start us, length us, event | category | flops | bytes accessed | tf_op | source)
XLA Modules:
  0.0 141.7 jit_solution(17487320557721707234)
XLA Ops:
  0.6 0.0 copy-start
  0.6 1.2 copy-done
  1.9 0.0 copy-start.1
  1.9 0.7 copy-done.1
  2.6 0.0 copy-start.2
  2.6 0.7 copy-done.2
  3.2 0.0 copy-start.3
  3.2 0.7 copy-done.3
  3.9 134.6 %shard_map.94 = (f32[8,8,32,256]{3,2,1,0:T(8,128)S(1)}, f32[8,8,32,256]{3,2,1,0:T(8,128)S(1)}, f32[1,32,128]{2,1,0:T(8,128)S(1)}) custom-call(s32[1,16]{1,0:T(1,128)S(1)} %copy-done.2, s32[32]{0:T(128)S(1)} %copy-done.3, f32[1,32,128]{2,1,0:T(8,128)S(1)} %copy-done.1, bf16[1,16,256,128]{3,2,1,0:T(8,128)(2,1)S(1)} %copy-done, f32[8,8,32,256]{3,2,1,0:T(8,128)} %bitcast.7, ...), custom_call_target="tpu_custom_call" | custom-call | flops 16999999488 | bytes 12000000 | tf_op jit(solution)/shard_map/pallas_call | solution.py:431
  138.5 1.3 copy.13
  139.8 1.3 copy.14
  141.1 0.6 copy.15
Async XLA Ops:
  0.6 1.2 copy-start
  1.9 0.7 copy-start.1
  2.6 0.7 copy-start.2
  3.2 0.7 copy-start.3

commit v3 on v2

--- a/solution.py
+++ b/solution.py
@@ -372,9 +372,8 @@
     lagged(0)
     gradient(0)
 
-    spread(1, 0, batches // 2)
+    spread(1, 0, batches)
     group_mean(0)
-    spread(1, batches // 2, batches)
     res_out[0] = residual(1)
     group_forward(0)
     group_close(0)

time: 145 us -> 144 us (level)
  no operation moved by 1% of the time
where the time goes in v3:
time: 144 us; the launch traced here: 142 us
  Pallas kernels  134 us (93%)
  local copies, waits for them, and re-layouts  6.49 us (5%)
    pallas_call x1, Pallas kernels, local(): pl.pallas_call(kernel, out_shape=(jax.ShapeDtypeStruct(split, F32), jax.S...  134 us
    unnamed x11, local copies, waits for them, and re-layouts  6.49 us

profile of v3, /device:TPU:2, one launch (start us, length us, event | category | flops | bytes accessed | tf_op | source)
XLA Modules:
  0.0 141.5 jit_solution(11251544750477116028)
XLA Ops:
  0.6 0.0 copy-start
  0.6 1.2 copy-done
  1.9 0.0 copy-start.1
  1.9 0.7 copy-done.1
  2.6 0.0 copy-start.2
  2.6 0.7 copy-done.2
  3.2 0.0 copy-start.3
  3.2 0.7 copy-done.3
  3.9 134.4 %shard_map.94 = (f32[8,8,32,256]{3,2,1,0:T(8,128)S(1)}, f32[8,8,32,256]{3,2,1,0:T(8,128)S(1)}, f32[1,32,128]{2,1,0:T(8,128)S(1)}) custom-call(s32[1,16]{1,0:T(1,128)S(1)} %copy-done.2, s32[32]{0:T(128)S(1)} %copy-done.3, f32[1,32,128]{2,1,0:T(8,128)S(1)} %copy-done.1, bf16[1,16,256,128]{3,2,1,0:T(8,128)(2,1)S(1)} %copy-done, f32[8,8,32,256]{3,2,1,0:T(8,128)} %bitcast.7, ...), custom_call_target="tpu_custom_call" | custom-call | flops 16999999488 | bytes 12000000 | tf_op jit(solution)/shard_map/pallas_call | solution.py:430
  138.3 1.3 copy.13
  139.6 1.3 copy.14
  140.9 0.6 copy.15
Async XLA Ops:
  0.6 1.2 copy-start
  1.9 0.7 copy-start.1
  2.6 0.7 copy-start.2
  3.2 0.7 copy-start.3
